TPU v7x, 32 devices: a whole 2x2x4 slice. The times are simulated.
32 devices in a mesh: dp: 8 (over z, y), co: 4 (over x, core).
Axes of the slice: x: 2, y: 2, z: 4, core: 2. Of those that a mesh axis runs over, the one named last changes fastest.
Arguments:
- embeddings: bfloat16 [3072, 1024], P(('dp', 'co')), may hold values from -2500 to 2500
- labels: int32 [3072], P(('dp', 'co')), may hold values from 0 to 63, as said below
- ranks: int32 [3072], P(('dp', 'co')), may hold values from 0 to 3071, each once
Outputs:
- max_cosine: float32 [3072], P(('dp', 'co'))
Inputs may be any that keep to these rules, and one draw needn't show every extreme that they name: The rows of one device hold at most 24 rows whose labels // 8 name one owner; in every draw some owner gets exactly 24 rows from every device.
All inputs are finite; a program needn't handle non-finite values.
Results may differ from a plain program's by a relative error of at most 0.00061.
Values may be sent and summed in bfloat16 or wider, within the bound.
A program may use at most 64 MiB of HBM per device.

v0:
```python
import jax
import jax.numpy as jnp
from jax import lax
from jax.sharding import PartitionSpec as P

CL_DEV = 8


EPSILON = 1e-06


def match_best(best, mine_rows, mine_label, mine_rank, other_rows, other_label, other_rank):
    scores = lax.dot_general(
        mine_rows, other_rows, (((1,), (1,)), ((), ())), preferred_element_type=jnp.float32
    )
    linked = (
        (mine_label[:, None] == other_label[None, :])
        & (other_label[None, :] >= 0)
        & (other_rank[None, :] < mine_rank[:, None])
    )
    return jnp.maximum(best, jnp.max(jnp.where(linked, scores, -1.0), axis=1))


def local(embeddings, labels, ranks):
    row_count, width = embeddings.shape
    owner_count = lax.axis_size("dp")
    slot_cap = max(2, 2 * row_count // owner_count)
    slot_total = owner_count * slot_cap
    values = embeddings.astype(jnp.float32)
    unit = (values * lax.rsqrt(jnp.sum(values * values, axis=1, keepdims=True) + EPSILON)).astype(
        jnp.bfloat16
    )
    owner = labels // CL_DEV
    onehot = (owner[:, None] == jnp.arange(owner_count, dtype=jnp.int32)[None, :]).astype(
        jnp.float32
    )
    lower = (jnp.arange(row_count)[:, None] >= jnp.arange(row_count)[None, :]).astype(jnp.float32)
    running = jnp.dot(lower, onehot, preferred_element_type=jnp.float32)
    position = (jnp.sum(running * onehot, axis=1) - 1.0).astype(jnp.int32)
    slot = owner * slot_cap + position
    send_rows = (
        jnp.zeros((slot_total, width), jnp.bfloat16)
        .at[slot]
        .set(unit)
        .reshape(owner_count, slot_cap, width)
    )
    send_label = (
        jnp.full((slot_total,), -1, jnp.int32).at[slot].set(labels).reshape(owner_count, slot_cap)
    )
    send_rank = (
        jnp.zeros((slot_total,), jnp.int32).at[slot].set(ranks).reshape(owner_count, slot_cap)
    )
    start_best = jnp.full((slot_total,), -1.0, jnp.float32)
    group_rows, group_label, group_rank = (
        lax.all_gather(send_rows, "co", axis=1, tiled=True),
        lax.all_gather(send_label, "co", axis=1, tiled=True),
        lax.all_gather(send_rank, "co", axis=1, tiled=True),
    )
    got_rows, got_label, got_rank = (
        lax.all_to_all(group_rows, "dp", split_axis=0, concat_axis=0, tiled=True),
        lax.all_to_all(group_label, "dp", split_axis=0, concat_axis=0, tiled=True),
        lax.all_to_all(group_rank, "dp", split_axis=0, concat_axis=0, tiled=True),
    )
    offset = lax.axis_index("co") * slot_cap
    mine_rows = lax.dynamic_slice_in_dim(got_rows, offset, slot_cap, 1).reshape(slot_total, width)
    mine_label = lax.dynamic_slice_in_dim(got_label, offset, slot_cap, 1).reshape(slot_total)
    mine_rank = lax.dynamic_slice_in_dim(got_rank, offset, slot_cap, 1).reshape(slot_total)
    best = match_best(
        start_best,
        mine_rows,
        mine_label,
        mine_rank,
        got_rows.reshape(-1, width),
        got_label.reshape(-1),
        got_rank.reshape(-1),
    )
    returned = lax.all_to_all(
        best.reshape(owner_count, slot_cap), "dp", split_axis=0, concat_axis=0, tiled=True
    )
    return returned.reshape(slot_total)[slot]


def solution(mesh):
    placed = (P(("dp", "co"), None), P(("dp", "co")), P(("dp", "co")))
    return jax.shard_map(
        local, mesh=mesh, in_specs=placed, out_specs=P(("dp", "co")), check_vma=False
    )
```

profile of v0, /device:TPU:0, one launch (start us, length us, event | category | flops | bytes accessed | tf_op | source)
XLA Modules:
  0.0 105.5 jit_solution(4677451876651736941)
XLA Ops:
  6.5 0.0 all-gather.4.cloned.1.call-start
  6.5 0.7 and_select_fusion
  7.2 0.1 fusion.1
  7.3 0.7 compare_select_fusion
  8.0 1.1 %fusion.2 = f32[96]{0:T(128)S(1)} fusion(bf16[96,1024]{1,0:T(8,128)(2,1)} %param.3), kind=kLoop, calls=%fused_computation.10 | loop fusion | flops 294816 | bytes 196992 | tf_op jit(solution)/shard_map/reduce_sum | solution.py:30
  9.1 2.2 %scatter_custom_fusion.2 = bf16[192,1024]{1,0:T(8,128)(2,1)} fusion(s32[96]{0:T(128)S(1)} %compare_select_fusion, bf16[96,1024]{1,0:T(8,128)(2,1)} %param.3, f32[96]{0:T(128)S(1)} %add_rsqrt_fusion, bf16[]{:T(256)} %constant.45.clone.1), kind=kCustom, calls=%fused_computation.12 | custom fusion | flops 294912 | bytes 590338 | tf_op jit(solution)/shard_map/scatter | solution.py:44
  11.3 0.0 all-gather.4.cloned.1.call-update
  11.4 1.0 scatter_custom_fusion.1
  12.4 0.1 reshape.65
  12.4 6.2 %all-gather.1 = s32[4,24,8]{1,2,0:T(8,128)S(1)} all-gather(s32[1,24,8]{1,2,0:T(8,128)S(1)} %bitcast.28), channel_id=1, replica_groups=mesh['dp'=8,'co'=4] {'co'}, dimensions={0}, use_global_device_ids=true | all-gather | bytes 3840 | tf_op jit(solution)/shard_map/all_gather | solution.py:57
  18.6 0.7 reshape.109
  19.3 6.3 %all-to-all-start.1 = ((s32[8,1,96]{2,1,0:T(1,128)}), s32[8,1,96]{2,1,0:T(1,128)S(1)}, u32[]{:S(2)}, u32[]{:S(2)}) async-start(s32[8,1,96]{2,1,0:T(1,128)} %bitcast.9), calls=%async_computation.1 | async-start | bytes 8192 | tf_op jit(solution)/shard_map/all_to_all | solution.py:62
  25.6 1.0 scatter_custom_fusion
  26.6 0.1 reshape.64
  26.7 5.2 %all-gather = s32[4,24,8]{1,2,0:T(8,128)S(1)} all-gather(s32[1,24,8]{1,2,0:T(8,128)S(1)} %bitcast.29), channel_id=1, replica_groups=mesh['dp'=8,'co'=4] {'co'}, dimensions={0}, use_global_device_ids=true | all-gather | bytes 3840 | tf_op jit(solution)/shard_map/all_gather | solution.py:56
  31.9 0.1 reshape.107
  32.0 0.1 all-to-all-done.1
  32.0 12.2 %all_to_all.29 = s32[8,1,96]{2,1,0:T(1,128)S(1)} all-to-all(s32[8,1,96]{2,1,0:T(1,128)S(1)} %bitcast.30), channel_id=1, replica_groups=mesh['dp'=8,'co'=4] {'dp'}, dimensions={0} | all-to-all | bytes 6144 | tf_op jit(solution)/shard_map/all_to_all | solution.py:61
  44.2 0.0 all-gather.4.cloned.1.call-done
  44.2 3.6 %all-to-all-start.2 = ((bf16[8,96,1024]{2,1,0:T(8,128)(2,1)}), bf16[8,96,1024]{2,1,0:T(8,128)(2,1)S(1)}, u32[]{:S(2)}, u32[]{:S(2)}) async-start(bf16[8,96,1024]{2,1,0:T(8,128)(2,1)} %all-gather.4.cloned.1.call-done), calls=%async_computation.2 | async-start | bytes 3145728 | tf_op jit(solution)/shard_map/all_to_all | solution.py:60
  47.8 0.5 broadcast.66
  48.3 0.7 reduce.17
  49.0 0.1 lt.30
  49.1 0.7 reduce.18
  49.7 0.1 eq.35
  49.8 0.1 dynamic-slice_reduce_fusion
  49.9 0.1 lt.32
  50.0 0.1 dynamic-slice_reduce_fusion.1
  50.1 0.1 eq.33
  50.2 33.9 %all-to-all-done.2 = bf16[8,96,1024]{2,1,0:T(8,128)(2,1)S(1)} async-done(((bf16[8,96,1024]{2,1,0:T(8,128)(2,1)}), bf16[8,96,1024]{2,1,0:T(8,128)(2,1)S(1)}, u32[]{:S(2)}, u32[]{:S(2)}) %all-to-all-start.2) | async-done | bytes 1572896 | tf_op jit(solution)/shard_map/all_to_all | solution.py:60
  84.1 0.8 fusion
  84.9 0.7 max_broadcast_in_dim.15
  85.6 3.6 %all-to-all-start.3 = ((f32[8,1,24]{2,1,0:T(1,128)}), f32[8,1,24]{2,1,0:T(1,128)S(1)}, u32[]{:S(2)}, u32[]{:S(2)}) async-start(f32[8,1,24]{2,1,0:T(1,128)} %max_broadcast_in_dim.15), calls=%async_computation.3 | async-start | bytes 8192 | tf_op jit(solution)/shard_map/all_to_all | solution.py:77
  89.2 6.5 %all-to-all-done.3 = f32[8,1,24]{2,1,0:T(1,128)S(1)} async-done(((f32[8,1,24]{2,1,0:T(1,128)}), f32[8,1,24]{2,1,0:T(1,128)S(1)}, u32[]{:S(2)}, u32[]{:S(2)}) %all-to-all-start.3) | async-done | bytes 800 | tf_op jit(solution)/shard_map/all_to_all | solution.py:77
  95.6 0.5 broadcast.68
  96.1 0.7 reduce.19
  96.8 0.1 reshape.69
  96.9 1.8 %gather_fusion = f32[96]{0:T(128)} fusion(f32[192]{0:T(256)S(1)} %reshape.69, s32[1024]{0:T(1024)S(1)} %pad_clamp_fusion), kind=kCustom, calls=%fused_computation | custom fusion | bytes 1152 | tf_op jit(solution)/shard_map/gather | solution.py:80
  (7 shorter events, 0.1 us)
Async XLA Ops:
  6.5 37.7 %all-gather.4.cloned.1.call-start = ((), (), s32[]{:S(2)}) async-start(), calls=%async_computation.4 | async-start | bytes 1966080 | tf_op jit(solution)/shard_map/all_gather | solution.py:55
  19.3 12.7 %all-to-all-start.1 = ((s32[8,1,96]{2,1,0:T(1,128)}), s32[8,1,96]{2,1,0:T(1,128)S(1)}, u32[]{:S(2)}, u32[]{:S(2)}) async-start(s32[8,1,96]{2,1,0:T(1,128)} %bitcast.9), calls=%async_computation.1 | async-start | bytes 8192 | tf_op jit(solution)/shard_map/all_to_all | solution.py:62
  44.2 39.8 %all-to-all-start.2 = ((bf16[8,96,1024]{2,1,0:T(8,128)(2,1)}), bf16[8,96,1024]{2,1,0:T(8,128)(2,1)S(1)}, u32[]{:S(2)}, u32[]{:S(2)}) async-start(bf16[8,96,1024]{2,1,0:T(8,128)(2,1)} %all-gather.4.cloned.1.call-done), calls=%async_computation.2 | async-start | bytes 3145728 | tf_op jit(solution)/shard_map/all_to_all | solution.py:60
  85.6 10.0 %all-to-all-start.3 = ((f32[8,1,24]{2,1,0:T(1,128)}), f32[8,1,24]{2,1,0:T(1,128)S(1)}, u32[]{:S(2)}, u32[]{:S(2)}) async-start(f32[8,1,24]{2,1,0:T(1,128)} %max_broadcast_in_dim.15), calls=%async_computation.3 | async-start | bytes 8192 | tf_op jit(solution)/shard_map/all_to_all | solution.py:77
Sparse Core Ops, SparseCore 0:
  11.5 22.4 all-gather.3
where the time goes:
time: 106 us; the launch traced here: 105 us
  waiting for transfers between devices  40.4 us (38%)
  blocking collectives  23.6 us (22%)
  between operations  13.5 us (13%)
  starting transfers between devices  13.4 us (13%)
  local copies, waits for them, and re-layouts  7 us (7%)
  other arithmetic  6.62 us (6%)
    all_to_all x1, waiting for transfers between devices, local(): lax.all_to_all(group_rows, 'dp', split_axis=0, concat_axis=0, tiled=True)  33.9 us
    all_to_all x1, blocking collectives, local(): lax.all_to_all(group_label, 'dp', split_axis=0, concat_axis=0, tiled=True)  12.2 us
    all_to_all x1, waiting for transfers between devices, local(): lax.all_to_all(best.reshape(owner_count, slot_cap), 'dp', split_axis=0, c...  6.46 us
    all_to_all x1, starting transfers between devices, local(): lax.all_to_all(group_rank, 'dp', split_axis=0, concat_axis=0, tiled=True)  6.28 us
    all_gather x1, blocking collectives, local(): lax.all_gather(send_rank, 'co', axis=1, tiled=True)  6.17 us
    all_gather x1, blocking collectives, local(): lax.all_gather(send_label, 'co', axis=1, tiled=True)  5.21 us
    all_to_all x1, starting transfers between devices, local(): lax.all_to_all(group_rows, 'dp', split_axis=0, concat_axis=0, tiled=True)  3.58 us
    all_to_all x1, starting transfers between devices, local(): lax.all_to_all(best.reshape(owner_count, slot_cap), 'dp', split_axis=0, c...  3.58 us
  transfers between devices with their start and end apart: 4, of which 3 were waited for; matrix products, arithmetic and copies ran while one was open for 5% of the time, Pallas kernels for 0%

commit v1 on v0

--- a/solution.py
+++ b/solution.py
@@ -1,6 +1,10 @@
+import functools
+
 import jax
 import jax.numpy as jnp
 from jax import lax
+from jax.experimental import pallas as pl
+from jax.experimental.pallas import tpu as pltpu
 from jax.sharding import PartitionSpec as P
 
 CL_DEV = 8
@@ -80,8 +84,297 @@
     return returned.reshape(slot_total)[slot]
 
 
+MESH = pl.DeviceIdType.MESH
+HIGHEST = lax.Precision.HIGHEST
+
+
+def iota(shape, dim):
+    return lax.broadcasted_iota(jnp.int32, shape, dim)
+
+
+def owner_place(owner, n_dp, n_co):
+    half = n_dp // 2
+    return n_dp // 4 + lax.rem(owner, half), (owner // half) * (n_co // 2)
+
+
+def kernel(
+    n_dp, n_co, cap, shift,
+    emb_ref, label_ref, rank_ref, out_ref,
+    send, recv, key_send, key_recv, rows, ret_send, ret_recv,
+    send_sem, recv_sem, key_send_sem, key_recv_sem, ret_send_sem, ret_recv_sem,
+):
+    n_dev = n_dp * n_co
+    n_owner = n_dp
+    row_count, width = emb_ref.shape
+    half = width // 2
+    total = n_dev * cap
+    my_dp, my_co = lax.axis_index("dp"), lax.axis_index("co")
+    me = my_dp * n_co + my_co
+    mid = n_dp // 4
+    is_owner = (my_dp >= mid) & (my_dp < mid + n_dp // 2) & (lax.rem(my_co, n_co // 2) == 0)
+    my_owner = (my_co // (n_co // 2)) * (n_dp // 2) + my_dp - mid
+
+    barrier = pltpu.get_barrier_semaphore()
+
+    def greet(j, _):
+        @pl.when(j != me)
+        def _():
+            pl.semaphore_signal(
+                barrier, inc=1, device_id=(j // n_co, lax.rem(j, n_co)), device_id_type=MESH
+            )
+        return 0
+
+    @pl.when(is_owner)
+    def _():
+        lax.fori_loop(0, n_dev, greet, 0)
+
+    @pl.when(jnp.logical_not(is_owner))
+    def _():
+        def greet_owner(o, _):
+            pl.semaphore_signal(
+                barrier, inc=1, device_id=owner_place(o, n_dp, n_co), device_id_type=MESH
+            )
+            return 0
+
+        lax.fori_loop(0, n_owner, greet_owner, 0)
+
+    values = emb_ref[...].astype(jnp.float32)
+    unit = (values * lax.rsqrt(jnp.sum(values * values, axis=1, keepdims=True) + EPSILON)).astype(
+        jnp.bfloat16
+    )
+    square = (row_count, row_count)
+    down, across = iota(square, 0), iota(square, 1)
+    label_row = label_ref[...]
+    key_row = label_row * (1 << shift) + rank_ref[...]
+    owner_row = label_row // CL_DEV
+    diagonal = down == across
+
+    def to_column(row):
+        return jnp.sum(jnp.where(diagonal, row, 0), axis=1, keepdims=True)
+
+    owner_col, key_col = to_column(owner_row), to_column(key_row)
+    same = owner_col == owner_row
+    place_row = jnp.sum(jnp.where(same & (down < across), 1, 0), axis=0, keepdims=True)
+    place_col = jnp.sum(jnp.where(same & (across < down), 1, 0), axis=1, keepdims=True)
+
+    @pl.when(is_owner)
+    def _():
+        pl.semaphore_wait(barrier, n_dev - 1)
+
+    @pl.when(jnp.logical_not(is_owner))
+    def _():
+        pl.semaphore_wait(barrier, n_owner)
+
+    def to_owner(step):
+        owner = lax.rem(me + step, n_owner)
+        dp, co = owner_place(owner, n_dp, n_co)
+        here = (dp == my_dp) & (co == my_co)
+        copies = [
+            pltpu.make_async_remote_copy(
+                src_ref=a.at[step], dst_ref=b.at[me], send_sem=x.at[step], recv_sem=y.at[me],
+                device_id=(dp, co), device_id_type=MESH,
+            )
+            for a, b, x, y in (
+                (key_send, key_recv, key_send_sem, key_recv_sem),
+                (send, recv, send_sem, recv_sem),
+            )
+        ]
+        local_copies = [
+            pltpu.make_async_copy(a.at[step], b.at[me], y.at[me])
+            for a, b, y in ((key_send, key_recv, key_recv_sem), (send, recv, recv_sem))
+        ]
+        return owner, here, copies, local_copies
+
+    lane = iota((row_count, 128), 1)
+    my_sublane = iota((8, 128), 0) == lax.rem(me, 8)
+    slot = iota((2 * cap, row_count), 0)
+    for step in range(n_owner):
+        owner, here, copies, local_copies = to_owner(step)
+        keys = jnp.sum(
+            jnp.where((owner_col == owner) & (place_col == lane), key_col + 1, 0),
+            axis=0, keepdims=True,
+        ) - 1
+        key_send[step] = jnp.where(my_sublane, keys, 0).astype(jnp.float32)
+        position = jnp.where(owner_row == owner, place_row, -2 * cap)
+        low = jnp.where(slot == position, 1.0, 0.0).astype(jnp.bfloat16)
+        high = jnp.where(slot == position + cap, 1.0, 0.0).astype(jnp.bfloat16)
+        picked = jnp.dot(low, unit[:, :half], preferred_element_type=jnp.float32) + jnp.dot(
+            high, unit[:, half:], preferred_element_type=jnp.float32
+        )
+        send[step] = picked.astype(jnp.bfloat16)
+
+        @pl.when(here)
+        def _():
+            for copy in local_copies:
+                copy.start()
+
+        @pl.when(jnp.logical_not(here))
+        def _():
+            for copy in copies:
+                copy.start()
+
+    @pl.when(is_owner)
+    def _():
+        every = iota((128, total), 1)
+        source = jnp.floor((every.astype(jnp.float32) + 0.5) * (1.0 / cap)).astype(jnp.int32)
+        spread = jnp.where(every - source * cap == iota((128, total), 0), 1.0, 0.0)
+        every_t = iota((total, 128), 0)
+        source_t = jnp.floor((every_t.astype(jnp.float32) + 0.5) * (1.0 / cap)).astype(jnp.int32)
+        spread_t = jnp.where(every_t - source_t * cap == iota((total, 128), 1), 1.0, 0.0)
+        from_row = source[:n_dev] == iota((n_dev, total), 0)
+        from_col = source_t[:, :n_dev] == iota((total, n_dev), 1)
+
+        def wait(kind, sem):
+            def one(j, _):
+                pltpu.make_async_copy(kind.at[j], kind.at[j], sem.at[j]).wait()
+                return 0
+
+            return one
+
+        lax.fori_loop(0, n_dev, wait(key_recv, key_recv_sem), 0)
+        table = jnp.sum(key_recv[...].reshape(n_dev // 8, 8, 8, 128), axis=1).reshape(n_dev, 128)
+        keys_row = jnp.sum(
+            jnp.where(
+                from_row,
+                jnp.dot(table, spread, precision=HIGHEST, preferred_element_type=jnp.float32),
+                0.0,
+            ),
+            axis=0, keepdims=True,
+        )
+        keys_col = jnp.sum(
+            jnp.where(
+                from_col,
+                lax.dot_general(
+                    spread_t, table, (((1,), (1,)), ((), ())),
+                    precision=HIGHEST, preferred_element_type=jnp.float32,
+                ),
+                0.0,
+            ),
+            axis=1, keepdims=True,
+        )
+        keys_row = jnp.round(keys_row)
+        keys_col = jnp.round(keys_col)
+        first_row = jnp.floor(keys_row * (1.0 / (1 << shift))) * (1 << shift)
+        first_row = jnp.maximum(first_row, 0.0)
+
+        for pair in range(n_dev // 2):
+            two = []
+            for j in (2 * pair, 2 * pair + 1):
+                pltpu.make_async_copy(recv.at[j], recv.at[j], recv_sem.at[j]).wait()
+                two.append(recv[j].astype(jnp.float32))
+            block = pl.ds(pair * 2 * cap, 2 * cap)
+            rows[block, :half] = jnp.concatenate([x[:cap] for x in two], axis=0).astype(jnp.bfloat16)
+            rows[block, half:] = jnp.concatenate([x[cap:] for x in two], axis=0).astype(jnp.bfloat16)
+
+        best = jnp.full((1, total), -1.0, jnp.float32)
+        tall = total // 3 if total % 48 == 0 else total
+        for begin in range(0, total, tall):
+            scores = lax.dot_general(
+                rows[begin : begin + tall, :], rows[...], (((1,), (1,)), ((), ())),
+                preferred_element_type=jnp.float32,
+            )
+            other = keys_col[begin : begin + tall]
+            linked = (other < keys_row) & (other >= first_row)
+            best = jnp.maximum(
+                best, jnp.max(jnp.where(linked, scores, -1.0), axis=0, keepdims=True)
+            )
+        ret_send[...] = lax.dot_general(
+            jnp.where(from_row, best, 0.0), spread, (((1,), (1,)), ((), ())),
+            precision=HIGHEST, preferred_element_type=jnp.float32,
+        ).reshape(n_dev // 8, 8, 128)
+
+        def back(j):
+            return pltpu.make_async_remote_copy(
+                src_ref=ret_send.at[j // 8], dst_ref=ret_recv.at[my_owner],
+                send_sem=ret_send_sem.at[j], recv_sem=ret_recv_sem.at[my_owner],
+                device_id=(j // n_co, lax.rem(j, n_co)), device_id_type=MESH,
+            )
+
+        def home(j):
+            return pltpu.make_async_copy(
+                ret_send.at[j // 8], ret_recv.at[my_owner], ret_recv_sem.at[my_owner]
+            )
+
+        def give(j, _):
+            @pl.when(j != me)
+            def _():
+                back(j).start()
+
+            @pl.when(j == me)
+            def _():
+                home(j).start()
+            return 0
+
+        lax.fori_loop(0, n_dev, give, 0)
+
+        def given(j, _):
+            @pl.when(j != me)
+            def _():
+                back(j).wait_send()
+            return 0
+
+        lax.fori_loop(0, n_dev, given, 0)
+
+    for step in range(n_owner):
+        _, here, copies, _ = to_owner(step)
+
+        @pl.when(jnp.logical_not(here))
+        def _():
+            for copy in copies:
+                copy.wait_send()
+
+    for o in range(n_owner):
+        pltpu.make_async_copy(ret_recv.at[o], ret_recv.at[o], ret_recv_sem.at[o]).wait()
+    mine = jnp.sum(jnp.where(my_sublane[None], ret_recv[...], 0.0), axis=1)
+    chosen = jnp.where(owner_row == iota((n_owner, row_count), 0), 1.0, 0.0)
+    by_place = lax.dot_general(
+        mine, chosen, (((0,), (0,)), ((), ())),
+        precision=HIGHEST, preferred_element_type=jnp.float32,
+    )
+    out_ref[...] = jnp.sum(
+        jnp.where(iota((128, row_count), 0) == place_row, by_place, 0.0), axis=0, keepdims=True
+    )
+
+
+def local_fused(n_dp, n_co, embeddings, labels, ranks):
+    row_count, width = embeddings.shape
+    cap = max(2, 2 * row_count // n_dp)
+    n_dev = n_dp * n_co
+    shift = (row_count * n_dev - 1).bit_length()
+    dma = pltpu.SemaphoreType.DMA
+    out = pl.pallas_call(
+        functools.partial(kernel, n_dp, n_co, cap, shift),
+        out_shape=jax.ShapeDtypeStruct((1, row_count), jnp.float32),
+        in_specs=[pl.BlockSpec(memory_space=pltpu.VMEM)] * 3,
+        out_specs=pl.BlockSpec(memory_space=pltpu.VMEM),
+        scratch_shapes=[
+            pltpu.VMEM((n_dp, 2 * cap, width // 2), jnp.bfloat16),
+            pltpu.VMEM((n_dev, 2 * cap, width // 2), jnp.bfloat16),
+            pltpu.VMEM((n_dp, 8, 128), jnp.float32),
+            pltpu.VMEM((n_dev, 8, 128), jnp.float32),
+            pltpu.VMEM((n_dev * cap, width), jnp.bfloat16),
+            pltpu.VMEM((n_dev // 8, 8, 128), jnp.float32),
+            pltpu.VMEM((n_dp, 8, 128), jnp.float32),
+            dma((n_dp,)), dma((n_dev,)), dma((n_dp,)), dma((n_dev,)), dma((n_dev,)), dma((n_dp,)),
+        ],
+        compiler_params=pltpu.CompilerParams(
+            collective_id=0, has_side_effects=True, vmem_limit_bytes=40 * 1024 * 1024
+        ),
+    )(embeddings, labels.reshape(1, row_count), ranks.reshape(1, row_count))
+    return out.reshape(row_count)
+
+
 def solution(mesh):
     placed = (P(("dp", "co"), None), P(("dp", "co")), P(("dp", "co")))
-    return jax.shard_map(
-        local, mesh=mesh, in_specs=placed, out_specs=P(("dp", "co")), check_vma=False
-    )
+    n_dp, n_co = mesh.shape["dp"], mesh.shape["co"]
+
+    def whole(embeddings, labels, ranks):
+        row_count = embeddings.shape[0] // (n_dp * n_co)
+        cap = max(2, 2 * row_count // n_dp)
+        fits = cap % 8 == 0 and cap <= 128 and n_dp % 4 == 0 and n_co % 2 == 0
+        body = functools.partial(local_fused, n_dp, n_co) if fits else local
+        return jax.shard_map(
+            body, mesh=mesh, in_specs=placed, out_specs=P(("dp", "co")), check_vma=False
+        )(embeddings, labels, ranks)
+
+    return whole

time: 106 us -> 29.9 us (0.28)
  waiting for transfers between devices: 40.4 us -> 0 us
  Pallas kernels: 0 us -> 27.6 us
  blocking collectives: 23.6 us -> 0 us
  between operations: 13.5 us -> 0.01 us
  starting transfers between devices: 13.4 us -> 0 us
  other arithmetic: 6.62 us -> 0 us
  local copies, waits for them, and re-layouts: 7 us -> 2.11 us
    all_to_all x3 -> x0, waiting for transfers between devices: 40.4 us -> none  [the longest x1 33.9 us: local(): lax.all_to_all(group_rows, 'dp', split_axis=0, concat_axis=0, tiled=True)]
    pallas_call x0 -> x1, Pallas kernels: none -> 27.6 us  [local_fused(): pl.pallas_call(functools.partial(kernel, n_dp, n_co, cap, shift), out_sha...]
    all_to_all x3 -> x0, starting transfers between devices: 13.4 us -> none  [the longest x1 6.28 us: local(): lax.all_to_all(group_rank, 'dp', split_axis=0, concat_axis=0, tiled=True)]
    all_to_all x1 -> x0, blocking collectives: 12.2 us -> none  [local(): lax.all_to_all(group_label, 'dp', split_axis=0, concat_axis=0, tiled=True)]
    all_gather x2 -> x0, blocking collectives: 11.4 us -> none  [the longest x1 6.17 us: local(): lax.all_gather(send_rank, 'co', axis=1, tiled=True)]
    scatter x1 -> x0, other arithmetic: 2.21 us -> none  [local(): send_rows = jnp.zeros((slot_total, width), jnp.bfloat16).at[slot].set(uni...]
    scatter x2 -> x0, local copies, waits for them, and re-layouts: 2.01 us -> none  [the longest x1 1 us: local(): jnp.zeros((slot_total,), jnp.int32).at[slot].set(ranks)]
    all_to_all x3 -> x0, other arithmetic: 1.98 us -> none  [the longest x1 0.66 us: local(): lax.all_to_all(group_label, 'dp', split_axis=0, concat_axis=0, tiled=True)]
  transfers between devices with their start and end apart: 4 -> 0, of which waited for: 3 -> 0; matrix products, arithmetic and copies ran while one was open for 5% -> 0% of each run, Pallas kernels for 0% -> 0%
where the time goes in v1:
time: 29.9 us; the launch traced here: 29.7 us
  Pallas kernels  27.6 us (92%)
  local copies, waits for them, and re-layouts  2.11 us (7%)
    pallas_call x1, Pallas kernels, local_fused(): pl.pallas_call(functools.partial(kernel, n_dp, n_co, cap, shift), out_sha...  27.6 us
    unnamed x7, local copies, waits for them, and re-layouts  2.11 us

profile of v1, /device:TPU:0, one launch (start us, length us, event | category | flops | bytes accessed | tf_op | source)
XLA Modules:
  0.0 29.7 jit_solution(4008433167096722868)
XLA Ops:
  0.0 0.0 copy-start.1
  0.0 0.0 copy-start.2
  0.0 0.7 %copy-done.1 = s32[96]{0:T(128)S(1)} copy-done((s32[96]{0:T(128)S(1)}, s32[96]{0:T(128)}, u32[]{:S(2)}) %copy-start.1) | copy-done | bytes 408
  0.7 0.0 copy-done.2
  0.7 0.0 copy-start
  0.7 0.9 %copy-done = bf16[96,1024]{1,0:T(8,128)(2,1)S(1)} copy-done((bf16[96,1024]{1,0:T(8,128)(2,1)S(1)}, bf16[96,1024]{1,0:T(8,128)(2,1)}, u32[]{:S(2)}) %copy-start) | copy-done | bytes 196632
  1.6 27.6 %shard_map.37 = f32[1,96]{1,0:T(1,128)S(1)} custom-call(bf16[96,1024]{1,0:T(8,128)(2,1)S(1)} %copy-done, s32[1,96]{1,0:T(1,128)S(1)} %bitcast.3, s32[1,96]{1,0:T(1,128)S(1)} %bitcast.4), custom_call_target="tpu_custom_call" | custom-call | tf_op jit(solution)/shard_map/pallas_call | solution.py:345
  29.2 0.5 %copy.5 = f32[96]{0:T(128)} copy(f32[96]{0:T(128)S(1)} %bitcast.5) | data formatting | bytes 768
Async XLA Ops:
  0.0 0.7 %copy-start.1 = (s32[96]{0:T(128)S(1)}, s32[96]{0:T(128)}, u32[]{:S(2)}) copy-start(s32[96]{0:T(128)} %param.4) | copy-start | bytes 1156
  0.0 0.7 %copy-start.2 = (s32[96]{0:T(128)S(1)}, s32[96]{0:T(128)}, u32[]{:S(2)}) copy-start(s32[96]{0:T(128)} %param.5) | copy-start | bytes 1156
  0.7 0.9 %copy-start = (bf16[96,1024]{1,0:T(8,128)(2,1)S(1)}, bf16[96,1024]{1,0:T(8,128)(2,1)}, u32[]{:S(2)}) copy-start(bf16[96,1024]{1,0:T(8,128)(2,1)} %emb_ref.1) | copy-start | bytes 589828

commit v2 on v1

--- a/solution.py
+++ b/solution.py
@@ -94,12 +94,13 @@
 
 def owner_place(owner, n_dp, n_co):
     half = n_dp // 2
-    return n_dp // 4 + lax.rem(owner, half), (owner // half) * (n_co // 2)
+    return n_dp // 4 + lax.rem(owner, half), (owner // half) * (n_co // 2) + 1
 
 
 def kernel(
     n_dp, n_co, cap, shift,
-    emb_ref, label_ref, rank_ref, out_ref,
+    emb_hbm, label_hbm, rank_hbm, out_ref,
+    emb_ref, label_ref, rank_ref, fetch_sem,
     send, recv, key_send, key_recv, rows, ret_send, ret_recv,
     send_sem, recv_sem, key_send_sem, key_recv_sem, ret_send_sem, ret_recv_sem,
 ):
@@ -111,9 +112,17 @@
     my_dp, my_co = lax.axis_index("dp"), lax.axis_index("co")
     me = my_dp * n_co + my_co
     mid = n_dp // 4
-    is_owner = (my_dp >= mid) & (my_dp < mid + n_dp // 2) & (lax.rem(my_co, n_co // 2) == 0)
+    is_owner = (my_dp >= mid) & (my_dp < mid + n_dp // 2) & (lax.rem(my_co, n_co // 2) == 1)
     my_owner = (my_co // (n_co // 2)) * (n_dp // 2) + my_dp - mid
 
+    fetches = [
+        pltpu.make_async_copy(a, b, fetch_sem.at[i])
+        for i, (a, b) in enumerate(
+            ((emb_hbm, emb_ref), (label_hbm, label_ref), (rank_hbm, rank_ref))
+        )
+    ]
+    for fetch in fetches:
+        fetch.start()
     barrier = pltpu.get_barrier_semaphore()
 
     def greet(j, _):
@@ -138,6 +147,8 @@
 
         lax.fori_loop(0, n_owner, greet_owner, 0)
 
+    for fetch in fetches:
+        fetch.wait()
     values = emb_ref[...].astype(jnp.float32)
     unit = (values * lax.rsqrt(jnp.sum(values * values, axis=1, keepdims=True) + EPSILON)).astype(
         jnp.bfloat16
@@ -156,14 +167,6 @@
     same = owner_col == owner_row
     place_row = jnp.sum(jnp.where(same & (down < across), 1, 0), axis=0, keepdims=True)
     place_col = jnp.sum(jnp.where(same & (across < down), 1, 0), axis=1, keepdims=True)
-
-    @pl.when(is_owner)
-    def _():
-        pl.semaphore_wait(barrier, n_dev - 1)
-
-    @pl.when(jnp.logical_not(is_owner))
-    def _():
-        pl.semaphore_wait(barrier, n_owner)
 
     def to_owner(step):
         owner = lax.rem(me + step, n_owner)
@@ -183,13 +186,13 @@
             pltpu.make_async_copy(a.at[step], b.at[me], y.at[me])
             for a, b, y in ((key_send, key_recv, key_recv_sem), (send, recv, recv_sem))
         ]
-        return owner, here, copies, local_copies
+        return here, copies, local_copies
 
     lane = iota((row_count, 128), 1)
     my_sublane = iota((8, 128), 0) == lax.rem(me, 8)
     slot = iota((2 * cap, row_count), 0)
     for step in range(n_owner):
-        owner, here, copies, local_copies = to_owner(step)
+        owner = lax.rem(me + step, n_owner)
         keys = jnp.sum(
             jnp.where((owner_col == owner) & (place_col == lane), key_col + 1, 0),
             axis=0, keepdims=True,
@@ -202,6 +205,17 @@
             high, unit[:, half:], preferred_element_type=jnp.float32
         )
         send[step] = picked.astype(jnp.bfloat16)
+
+    @pl.when(is_owner)
+    def _():
+        pl.semaphore_wait(barrier, n_dev - 1)
+
+    @pl.when(jnp.logical_not(is_owner))
+    def _():
+        pl.semaphore_wait(barrier, n_owner)
+
+    for step in range(n_owner):
+        here, copies, local_copies = to_owner(step)
 
         @pl.when(here)
         def _():
@@ -316,7 +330,7 @@
         lax.fori_loop(0, n_dev, given, 0)
 
     for step in range(n_owner):
-        _, here, copies, _ = to_owner(step)
+        here, copies, _ = to_owner(step)
 
         @pl.when(jnp.logical_not(here))
         def _():
@@ -345,9 +359,13 @@
     out = pl.pallas_call(
         functools.partial(kernel, n_dp, n_co, cap, shift),
         out_shape=jax.ShapeDtypeStruct((1, row_count), jnp.float32),
-        in_specs=[pl.BlockSpec(memory_space=pltpu.VMEM)] * 3,
+        in_specs=[pl.BlockSpec(memory_space=pltpu.HBM)] * 3,
         out_specs=pl.BlockSpec(memory_space=pltpu.VMEM),
         scratch_shapes=[
+            pltpu.VMEM((row_count, width), jnp.bfloat16),
+            pltpu.VMEM((1, row_count), jnp.int32),
+            pltpu.VMEM((1, row_count), jnp.int32),
+            dma((3,)),
             pltpu.VMEM((n_dp, 2 * cap, width // 2), jnp.bfloat16),
             pltpu.VMEM((n_dev, 2 * cap, width // 2), jnp.bfloat16),
             pltpu.VMEM((n_dp, 8, 128), jnp.float32),
@@ -358,7 +376,7 @@
             dma((n_dp,)), dma((n_dev,)), dma((n_dp,)), dma((n_dev,)), dma((n_dev,)), dma((n_dp,)),
         ],
         compiler_params=pltpu.CompilerParams(
-            collective_id=0, has_side_effects=True, vmem_limit_bytes=40 * 1024 * 1024
+            collective_id=0, has_side_effects=True, vmem_limit_bytes=63 * 1024 * 1024
         ),
     )(embeddings, labels.reshape(1, row_count), ranks.reshape(1, row_count))
     return out.reshape(row_count)
@@ -371,7 +389,7 @@
     def whole(embeddings, labels, ranks):
         row_count = embeddings.shape[0] // (n_dp * n_co)
         cap = max(2, 2 * row_count // n_dp)
-        fits = cap % 8 == 0 and cap <= 128 and n_dp % 4 == 0 and n_co % 2 == 0
+        fits = cap % 8 == 0 and cap <= 128 and n_dp % 4 == 0 and n_co % 4 == 0
         body = functools.partial(local_fused, n_dp, n_co) if fits else local
         return jax.shard_map(
             body, mesh=mesh, in_specs=placed, out_specs=P(("dp", "co")), check_vma=False

time: 29.9 us -> 28.4 us (0.950)
  local copies, waits for them, and re-layouts: 2.11 us -> 1.1 us
  Pallas kernels: 27.6 us -> 27.2 us
    unnamed x7 -> x3, local copies, waits for them, and re-layouts: 2.11 us -> 1.1 us
    pallas_call x1, Pallas kernels: 27.6 us -> 27.2 us  [local_fused(): pl.pallas_call(functools.partial(kernel, n_dp, n_co, cap, shift), out_sha...]
where the time goes in v2:
time: 28.4 us; the launch traced here: 28.3 us
  Pallas kernels  27.2 us (96%)
  local copies, waits for them, and re-layouts  1.1 us (4%)
    pallas_call x1, Pallas kernels, local_fused(): pl.pallas_call(functools.partial(kernel, n_dp, n_co, cap, shift), out_sha...  27.2 us
    unnamed x3, local copies, waits for them, and re-layouts  1.1 us

profile of v2, /device:TPU:0, one launch (start us, length us, event | category | flops | bytes accessed | tf_op | source)
XLA Modules:
  0.0 28.3 jit_solution(12536481355279178319)
XLA Ops:
  0.0 27.2 %shard_map.37 = f32[1,96]{1,0:T(1,128)} custom-call(bf16[96,1024]{1,0:T(8,128)(2,1)} %emb_hbm.1, s32[1,96]{1,0:T(1,128)} %bitcast.3, s32[1,96]{1,0:T(1,128)} %bitcast.4), custom_call_target="tpu_custom_call" | custom-call | tf_op jit(solution)/shard_map/pallas_call | solution.py:359
  27.2 0.0 copy-start
  27.2 0.6 %copy-done = f32[1,96]{1,0:T(1,128)S(1)} copy-done((f32[1,96]{1,0:T(1,128)S(1)}, f32[1,96]{1,0:T(1,128)}, u32[]{:S(2)}) %copy-start) | copy-done | bytes 408
  27.8 0.5 %copy.5 = f32[96]{0:T(128)} copy(f32[96]{0:T(128)S(1)} %bitcast.5) | data formatting | bytes 768
Async XLA Ops:
  27.2 0.6 %copy-start = (f32[1,96]{1,0:T(1,128)S(1)}, f32[1,96]{1,0:T(1,128)}, u32[]{:S(2)}) copy-start(f32[1,96]{1,0:T(1,128)} %shard_map.37) | copy-start | bytes 1156
